TPU v7x, 512 devices: a whole 4x8x8 slice. The times are simulated.
512 devices in a mesh: child: 2 (over x_hi), row: 16 (over z, x_lo), col: 16 (over y, core).
Axes of the slice: x: 4 (x_hi: 2, x_lo: 2; x = x_hi * 2 + x_lo), y: 8, z: 8, core: 2. Of those that a mesh axis runs over, the one named last changes fastest.
Arguments:
- contrib: float32 [2, 8192, 8192], P('child', 'row', 'col'), may hold values from -0.0625 to 0.0625
- assembled: float32 [2, 8192, 16384], P('child', 'row', 'col'), may hold values from -0.0625 to 0.0625
- pattern: int32 [64, 64], P('row', 'col'), may hold values 0 or 1
- omega: float32 [16384, 256], P('col', 'row'), may hold values from -6 to 6
- row_maps: int32 [2, 8192], P('child'), may hold values from 0 to 16383, as said below
- leaf_bounds: int32 [16], P('row'), may hold values from 448 to 576
Outputs:
- bases: float32 [16384, 256], P('row', ('child', 'col'))
- coupling: float32 [16, 2, 256, 256], P('row', None, ('child', 'col'))
Inputs may be any that keep to these rules, and one draw needn't show every extreme that they name: `row_maps`: for each child, entries k * 512 to (k + 1) * 512 - 1 are distinct, rising, and lie in k * 1024 to (k + 1) * 1024 - 1.
All inputs are finite; a program needn't handle non-finite values. No bound on the sum of `pattern` on one device may be relied on, other than what follows from the above.
Results may differ from a plain program's by a relative error of at most 0.0003.
Values sent between devices are 32-bit elements; how exact they have to be, the bound alone decides.
No kernel may reach another device: no remote copies, remote signals or barrier semaphores. Data moves between devices by JAX's collectives and lax.ppermute only.
A program may use at most 64 MiB of HBM per device.

v0:
```python
import jax
import jax.numpy as jnp
from jax import lax
from jax.sharding import PartitionSpec as P

R = 256
BT = 256
highest = lax.Precision.HIGHEST


def partner(block, axis, distance):
    count = lax.axis_size(axis)
    route = []
    for low in range(count):
        high = low | 1 << distance
        if high != low and high < count:
            route += [(low, high), (high, low)]
    return lax.ppermute(block, axis, route)


def window_leaves(window, leaf_bound, counts):
    window_rows = window.shape[0]
    upper = window_rows // 2 + window_rows // 16
    lower = window_rows // 2 - window_rows // 16
    positions = jnp.arange(window_rows, dtype=jnp.int32)
    first_leaf = (positions < leaf_bound)[:, None]
    head_rows = window[:upper]
    tail_rows = window[lower:]
    head_masked = jnp.where(first_leaf[:upper], head_rows, 0.0)
    tail_masked = jnp.where(first_leaf[lower:], 0.0, tail_rows)
    head_gram = jnp.dot(head_masked.T, head_rows, precision=highest)
    tail_gram = jnp.dot(tail_masked.T, tail_rows, precision=highest)
    factors = jnp.linalg.cholesky(jnp.stack([head_gram, tail_gram]) / counts)
    head_part = lax.linalg.triangular_solve(
        factors[0], head_rows, left_side=False, lower=True, transpose_a=True
    )
    tail_part = lax.linalg.triangular_solve(
        factors[1], tail_rows, left_side=False, lower=True, transpose_a=True
    )
    middle = jnp.where(first_leaf[lower:upper], head_part[lower:], tail_part[: upper - lower])
    whole = jnp.concatenate([head_part[:lower], middle, tail_part[upper - lower :]], axis=0)
    return (factors, whole)


def local(contrib, assembled, pattern, omega, row_maps, leaf_bounds):
    tile_rows = contrib.shape[1]
    tile_cols = contrib.shape[2]
    window_rows = omega.shape[0]
    slice_width = R // (2 * lax.axis_size("col"))
    row_pos = lax.axis_index("row")
    col_pos = lax.axis_index("col")
    half_pos = lax.axis_index("child")
    group_pos = half_pos * lax.axis_size("col") + col_pos
    zero_index = jnp.zeros((), jnp.int32)
    child_maps = row_maps[0]
    column_maps = (
        lax.dynamic_slice_in_dim(child_maps, col_pos * tile_cols, tile_cols) - col_pos * window_rows
    )
    target_maps = (
        lax.dynamic_slice_in_dim(child_maps, row_pos * tile_rows, tile_rows) - row_pos * window_rows
    )
    full_omega = lax.all_gather(omega, "row", axis=1, tiled=True)
    picked = jnp.take(full_omega, column_maps, axis=0)
    product = jnp.dot(contrib[0], picked, precision=highest)
    pattern_rows = lax.dynamic_slice_in_dim(
        pattern, half_pos * (tile_rows // BT), tile_rows // BT, 0
    ).astype(jnp.float32)
    masked = (
        assembled[0].reshape(tile_rows // BT, BT, window_rows // BT, BT)
        * pattern_rows[:, None, :, None]
    ).reshape(tile_rows, window_rows)
    sparse = jnp.dot(masked, full_omega, precision=highest)
    child_red, sparse_red = (
        lax.psum_scatter(
            product.reshape(tile_rows, 2, R // 2), "col", scatter_dimension=2, tiled=True
        ),
        lax.psum_scatter(
            sparse.reshape(tile_rows, 2, R // 2), "col", scatter_dimension=2, tiled=True
        ),
    )
    spread = jnp.zeros((window_rows, 2, slice_width), jnp.float32).at[target_maps].add(child_red)
    placed = lax.dynamic_update_slice(
        jnp.zeros((window_rows, 2, slice_width), jnp.float32),
        sparse_red,
        (half_pos * tile_rows, zero_index, zero_index),
    )
    samples = lax.psum_scatter(spread + placed, "child", scatter_dimension=1, tiled=True).reshape(
        window_rows, slice_width
    )
    leaf_bound = leaf_bounds[0]
    head_count = leaf_bound.astype(jnp.float32)
    tail_count = (window_rows - leaf_bound).astype(jnp.float32)
    counts = jnp.stack([head_count, tail_count])[:, None, None]
    window = lax.all_gather(samples, ("child", "col"), axis=1, tiled=True)
    factors, whole = window_leaves(window, leaf_bound, counts)
    bases = lax.dynamic_slice_in_dim(whole, group_pos * slice_width, slice_width, 1)
    own_cols = lax.dynamic_slice_in_dim(factors, group_pos * slice_width, slice_width, 2)
    sibling = partner(factors, "row", 0)
    coupling = jnp.einsum("lab,lac->lbc", own_cols, sibling, precision=highest)
    return (bases, coupling[None])


def solution(mesh):
    in_specs = (
        P("child", "row", "col"),
        P("child", "row", "col"),
        P("row", "col"),
        P("col", "row"),
        P("child", None),
        P("row"),
    )
    out_specs = (P("row", ("child", "col")), P("row", None, ("child", "col"), None))
    return jax.shard_map(local, mesh=mesh, in_specs=in_specs, out_specs=out_specs, check_vma=False)
```

profile of v0, /device:TPU:1, one launch (start us, length us, event | category | flops | bytes accessed | tf_op | source)
XLA Modules:
  0.0 525.0 jit_solution(18265540738242747835)
XLA Ops:
  9.0 2.1 mul.46
  11.9 65.8 %all-gather.4.cloned.1.call-done = f32[1024,256]{0,1:T(8,128)} async-done(((f32[1024,16]{0,1:T(8,128)}), f32[1024,256]{0,1:T(8,128)}) %all-gather.4.cloned.1.call-update) | async-done | bytes 1048592 | tf_op jit(solution)/shard_map/all_gather | solution.py:62
  77.6 1.6 copy.55
  79.2 2.2 gather_fusion
  81.5 3.1 fusion.3
  85.9 4.7 fusion
  90.7 1.3 dynamic-slice.8
  92.6 118.2 %all-reduce.4.cloned.1.call-done = f32[512,2,128]{0,1,2:T(2,128)} async-done(((f32[512,2,128]{0,1,2:T(2,128)}), f32[512,2,128]{0,1,2:T(2,128)}) %all-reduce.4.cloned.1.call-update) | async-done | bytes 524304
  212.1 16.7 %scatter_fusion = f32[1024,2,8]{2,1,0:T(2,128)S(1)} fusion(f32[1024,2,8]{2,1,0:T(2,128)S(1)} %broadcast.161, s32[512]{0:T(512)S(1)} %bitcast.118, f32[512,2,8]{2,1,0:T(2,128)S(1)} %copy.57), kind=kCustom, calls=%fused_computation.1 | custom fusion | flops 8192 | bytes 100352 | tf_op jit(solution)/shard_map/scatter-add | solution.py:81
  229.0 42.9 %reduce-scatter.3.cloned.1.call-done = f32[512,2,8]{0,2,1:T(8,128)} async-done(((f32[512,2,128]{0,2,1:T(8,128)}), f32[512,2,8]{0,2,1:T(8,128)}) %reduce-scatter.3.cloned.1.call-update) | async-done | bytes 32784 | tf_op jit(solution)/shard_map/reduce_scatter | solution.py:77
  274.3 19.7 %reduce-scatter.5.cloned.1.call-done = f32[1024,1,8]{0,2,1:T(8,128)} async-done(((f32[1024,2,8]{0,2,1:T(8,128)}), f32[1024,1,8]{0,2,1:T(8,128)}) %reduce-scatter.5.cloned.1.call-update) | async-done | bytes 32784 | tf_op jit(solution)/shard_map/reduce_scatter | solution.py:87
  294.0 1.4 copy.61
  296.4 84.6 %all-gather.6.cloned.1.call-done = f32[1024,1,256]{0,1,2:T(1,128)} async-done(((f32[1024,1,8]{0,1,2:T(1,128)}), f32[1024,1,256]{0,1,2:T(1,128)}) %all-gather.6.cloned.1.call-update) | async-done | bytes 1048592 | tf_op jit(solution)/shard_map/all_gather | solution.py:94
  381.1 3.1 fusion.48
  385.0 1.3 convolution_bitcast_fusion
  386.4 1.3 convolution_bitcast_fusion.1
  388.6 1.2 copy.66
  390.8 23.5 %custom-call.16 = f32[2,128,128]{2,1,0:T(8,128)S(1)} custom-call(f32[2,128,128]{2,1,0:T(8,128)S(1)} %cholesky.122), custom_call_target="Cholesky" | custom-call | tf_op jit(solution)/shard_map/jit(cholesky)/cholesky | solution.py:33
  414.3 19.7 %custom-call.17 = f32[2,1,128,128]{2,3,1,0:T(8,128)S(1)} custom-call(f32[2,1,128,128]{3,2,1,0:T(8,128)S(1)} %select_bitcast_fusion), custom_call_target="InvertDiagBlocksLowerTriangular" | custom-call | tf_op jit(solution)/shard_map/jit(cholesky)/cholesky | solution.py:33
  435.2 1.3 convolution_subtract_fusion.2
  436.5 23.7 %custom-call.18 = f32[2,128,128]{2,1,0:T(8,128)S(1)} custom-call(f32[2,128,128]{2,1,0:T(8,128)S(1)} %convolution_subtract_fusion.2), custom_call_target="Cholesky" | custom-call | tf_op jit(solution)/shard_map/jit(cholesky)/cholesky | solution.py:33
  460.6 2.2 collective-permute-start
  462.9 4.0 while.4
  463.5 1.4 bitcast_dynamic-update-slice_fusion.4
  465.5 1.4 bitcast_dynamic-update-slice_fusion.4
  467.5 20.5 %custom-call.20 = f32[2,128,128]{1,2,0:T(8,128)S(1)} custom-call(f32[2,128,128]{2,1,0:T(8,128)} %copy-done.4), custom_call_target="InvertDiagBlocksLowerTriangular" | custom-call | tf_op jit(solution)/shard_map/triangular_solve/custom-call.0 | solution.py:34
  488.4 1.2 convolution_subtract_fusion.1
  490.1 4.0 while.5
  490.7 1.4 bitcast_dynamic-update-slice_fusion.5
  492.7 1.4 bitcast_dynamic-update-slice_fusion.5
  494.1 19.7 %custom-call.21 = f32[2,128,128]{1,2,0:T(8,128)S(1)} custom-call(f32[2,128,128]{2,1,0:T(8,128)S(1)} %get-tuple-element.18), custom_call_target="InvertDiagBlocksLowerTriangular" | custom-call | tf_op jit(solution)/shard_map/triangular_solve/custom-call.0 | solution.py:37
  516.2 2.3 convolution_bitcast_fusion.2
  (77 shorter events, 18.5 us)
Async XLA Ops:
  7.2 74.3 %copy-start = (f32[1,512,512]{2,1,0:T(8,128)S(1)}, f32[1,512,512]{2,1,0:T(8,128)}, u32[]{:S(2)}) copy-start(f32[1,512,512]{2,1,0:T(8,128)} %param.8) | copy-start | bytes 3145732
  7.2 70.5 %all-gather.4.cloned.1.call-start = ((), (), s32[]{:S(2)}) async-start(), calls=%async_computation.2 | async-start | bytes 1114112 | tf_op jit(solution)/shard_map/all_gather | solution.py:62
  7.9 202.9 %all-reduce.4.cloned.1.call-start = ((), (), s32[]{:S(2)}) async-start(), calls=%async_computation.6 | async-start | bytes 1048576
  81.5 4.4 copy-start.1
  85.8 186.1 %reduce-scatter.3.cloned.1.call-start = ((), (), s32[]{:S(2)}) async-start(), calls=%async_computation.3 | async-start | bytes 557056 | tf_op jit(solution)/shard_map/reduce_scatter | solution.py:77
  90.6 203.4 %reduce-scatter.5.cloned.1.call-start = ((), (), s32[]{:S(2)}) async-start(), calls=%async_computation.4 | async-start | bytes 98304 | tf_op jit(solution)/shard_map/reduce_scatter | solution.py:87
  274.1 107.0 %all-gather.6.cloned.1.call-start = ((), (), s32[]{:S(2)}) async-start(), calls=%async_computation.5 | async-start | bytes 1081344 | tf_op jit(solution)/shard_map/all_gather | solution.py:94
  390.0 0.8 copy-start.3
  460.6 55.6 %collective-permute-start = (f32[2,256,256]{2,1,0:T(8,128)S(1)}, f32[2,256,256]{2,1,0:T(8,128)}, u32[]{:S(2)}, u32[]{:S(2)}) collective-permute-start(f32[2,256,256]{2,1,0:T(8,128)S(1)} %select_select_fusion), channel_id=1, source_target_pairs={{0,16},{16,0},{32,48},{48,32},{64,80},{80,64},{96,112},{112,96},{1... | collective-permute-start | bytes 1572872 | tf_op jit(solution)/shard_map/ppermute | solution.py:18
  466.8 0.7 copy-start.4
  467.5 20.5 %copy-start.2 = (f32[256,256]{1,0:T(8,128)}, f32[256,256]{1,0:T(8,128)S(1)}, u32[]{:S(2)}) copy-start(f32[256,256]{1,0:T(8,128)S(1)} %get-tuple-element.164) | copy-start | bytes 786436
Sparse Core Ops, SparseCore 0:
  10.1 67.5 all-gather.3
  86.0 124.8 all-reduce.3
  213.9 57.9 reduce-scatter.2
  274.5 19.4 reduce-scatter.4
  297.8 83.2 all-gather.5
where the time goes:
time: 526 us; the launch traced here: 525 us
  waiting for transfers between devices  332 us (63%)
  other arithmetic  128 us (24%)
  local copies, waits for them, and re-layouts  28.5 us (5%)
  matrix products  18.5 us (4%)
  between operations  15.5 us (3%)
    unnamed x6, waiting for transfers between devices  119 us
    all_gather x1, waiting for transfers between devices, local(): window = lax.all_gather(samples, ('child', 'col'), axis=1, tiled=True)  84.6 us
    another operation x9, other arithmetic, window_leaves(): factors = jnp.linalg.cholesky(jnp.stack([head_gram, tail_gram]) / counts)  67.1 us
    all_gather x1, waiting for transfers between devices, local(): full_omega = lax.all_gather(omega, 'row', axis=1, tiled=True)  65.8 us
    reduce_scatter x1, waiting for transfers between devices, local(): lax.psum_scatter(sparse.reshape(tile_rows, 2, R // 2), 'col', scatter_dim...  42.9 us
    another operation x4, other arithmetic, window_leaves(): lax.linalg.triangular_solve(factors[0], head_rows, left_side=False, lower...  20.6 us
    reduce_scatter x1, waiting for transfers between devices, local(): lax.psum_scatter(spread + placed, 'child', scatter_dimension=1, tiled=True)  19.7 us
    another operation x2, other arithmetic, window_leaves(): lax.linalg.triangular_solve(factors[1], tail_rows, left_side=False, lower...  19.7 us
  transfers between devices with their start and end apart: 6, of which 5 were waited for; matrix products, arithmetic and copies ran while one was open for 15% of the time, Pallas kernels for 0%

commit v1 on v0

--- a/solution.py
+++ b/solution.py
@@ -59,7 +59,10 @@
     target_maps = (
         lax.dynamic_slice_in_dim(child_maps, row_pos * tile_rows, tile_rows) - row_pos * window_rows
     )
-    full_omega = lax.all_gather(omega, "row", axis=1, tiled=True)
+    n_dev = lax.axis_size("row")
+    blocks = jnp.stack([omega for _ in range(n_dev)])
+    blocks = lax.all_to_all(blocks, "row", split_axis=0, concat_axis=0)
+    full_omega = jnp.concatenate(blocks, axis=1)
     picked = jnp.take(full_omega, column_maps, axis=0)
     product = jnp.dot(contrib[0], picked, precision=highest)
     pattern_rows = lax.dynamic_slice_in_dim(

time: 526 us -> 484 us (0.920)
  waiting for transfers between devices: 332 us -> 275 us
  starting transfers between devices: 2.58 us -> 14.4 us
    all_gather x1 -> x0, waiting for transfers between devices: 65.8 us -> none  [local(): full_omega = lax.all_gather(omega, 'row', axis=1, tiled=True)]
    all_to_all x0 -> x1, waiting for transfers between devices: none -> 19.5 us  [local(): blocks = lax.all_to_all(blocks, 'row', split_axis=0, concat_axis=0)]
    all_to_all x0 -> x1, starting transfers between devices: none -> 11.9 us  [local(): blocks = lax.all_to_all(blocks, 'row', split_axis=0, concat_axis=0)]
    unnamed x6 -> x5, waiting for transfers between devices: 119 us -> 108 us
  transfers between devices with their start and end apart: 6 -> 6, of which waited for: 5 -> 5; matrix products, arithmetic and copies ran while one was open for 15% -> 17% of each run, Pallas kernels for 0% -> 0%
where the time goes in v1:
time: 484 us; the launch traced here: 483 us
  waiting for transfers between devices  275 us (57%)
  other arithmetic  127 us (26%)
  local copies, waits for them, and re-layouts  31.8 us (7%)
  matrix products  18.7 us (4%)
  between operations  15.5 us (3%)
  starting transfers between devices  14.4 us (3%)
    unnamed x5, waiting for transfers between devices  108 us
    all_gather x1, waiting for transfers between devices, local(): window = lax.all_gather(samples, ('child', 'col'), axis=1, tiled=True)  84.7 us
    another operation x9, other arithmetic, window_leaves(): factors = jnp.linalg.cholesky(jnp.stack([head_gram, tail_gram]) / counts)  67.1 us
    reduce_scatter x1, waiting for transfers between devices, local(): lax.psum_scatter(sparse.reshape(tile_rows, 2, R // 2), 'col', scatter_dim...  42.9 us
    another operation x4, other arithmetic, window_leaves(): lax.linalg.triangular_solve(factors[0], head_rows, left_side=False, lower...  20.6 us
    reduce_scatter x1, waiting for transfers between devices, local(): lax.psum_scatter(spread + placed, 'child', scatter_dimension=1, tiled=True)  19.9 us
    another operation x2, other arithmetic, window_leaves(): lax.linalg.triangular_solve(factors[1], tail_rows, left_side=False, lower...  19.7 us
    all_to_all x1, waiting for transfers between devices, local(): blocks = lax.all_to_all(blocks, 'row', split_axis=0, concat_axis=0)  19.5 us
  transfers between devices with their start and end apart: 6, of which 5 were waited for; matrix products, arithmetic and copies ran while one was open for 17% of the time, Pallas kernels for 0%

profile of v1, /device:TPU:1, one launch (start us, length us, event | category | flops | bytes accessed | tf_op | source)
XLA Modules:
  0.0 482.9 jit_solution(6069594886435231908)
XLA Ops:
  7.2 2.0 stack.14
  9.2 11.9 %all-to-all-start = ((f32[16,1024,16]{1,2,0:T(8,128)}), f32[16,1024,16]{1,2,0:T(8,128)S(1)}, u32[]{:S(2)}, u32[]{:S(2)}) async-start(f32[16,1024,16]{1,2,0:T(8,128)} %stack.14), calls=%async_computation | async-start | bytes 2097152 | tf_op jit(solution)/shard_map/all_to_all | solution.py:64
  21.2 1.6 mul.45
  22.8 3.3 mul.46
  26.9 19.5 %all-to-all-done = f32[16,1024,16]{1,2,0:T(8,128)S(1)} async-done(((f32[16,1024,16]{1,2,0:T(8,128)}), f32[16,1024,16]{1,2,0:T(8,128)S(1)}, u32[]{:S(2)}, u32[]{:S(2)}) %all-to-all-start) | async-done | bytes 1048608 | tf_op jit(solution)/shard_map/all_to_all | solution.py:64
  46.7 2.2 gather_fusion
  49.0 3.0 fusion.3
  53.3 5.1 %fusion = f32[512,2,128]{0,2,1:T(8,128)} fusion(f32[2,128,1024]{2,1,0:T(8,128)S(1)} %bitcast.117, f32[1,512,1024]{2,1,0:T(8,128)} %param.9, f32[1,512,1024]{2,1,0:T(8,128)} %mul.46), kind=kOutput, calls=%fused_computation.6 | convolution fusion | flops 1611137024 | bytes 5767168 | tf_op jit(solution)/shard_map/dot_general | solution.py:75
  58.4 1.3 dynamic-slice.8
  60.4 108.3 %all-reduce.4.cloned.1.call-done = f32[512,2,128]{0,1,2:T(2,128)} async-done(((f32[512,2,128]{0,1,2:T(2,128)}), f32[512,2,128]{0,1,2:T(2,128)}) %all-reduce.4.cloned.1.call-update) | async-done | bytes 524304
  169.9 16.7 %scatter_fusion = f32[1024,2,8]{2,1,0:T(2,128)S(1)} fusion(f32[1024,2,8]{2,1,0:T(2,128)S(1)} %broadcast.163, s32[512]{0:T(512)S(1)} %bitcast.123, f32[512,2,8]{2,1,0:T(2,128)S(1)} %copy.56), kind=kCustom, calls=%fused_computation.1 | custom fusion | flops 8192 | bytes 100352 | tf_op jit(solution)/shard_map/scatter-add | solution.py:84
  186.8 42.9 %reduce-scatter.3.cloned.1.call-done = f32[512,2,8]{0,2,1:T(8,128)} async-done(((f32[512,2,128]{0,2,1:T(8,128)}), f32[512,2,8]{0,2,1:T(8,128)}) %reduce-scatter.3.cloned.1.call-update) | async-done | bytes 32784 | tf_op jit(solution)/shard_map/reduce_scatter | solution.py:80
  232.1 19.9 %reduce-scatter.5.cloned.1.call-done = f32[1024,1,8]{0,2,1:T(8,128)} async-done(((f32[1024,2,8]{0,2,1:T(8,128)}), f32[1024,1,8]{0,2,1:T(8,128)}) %reduce-scatter.5.cloned.1.call-update) | async-done | bytes 32784 | tf_op jit(solution)/shard_map/reduce_scatter | solution.py:90
  251.9 1.4 copy.60
  254.3 84.7 %all-gather.3.cloned.1.call-done = f32[1024,1,256]{0,1,2:T(1,128)} async-done(((f32[1024,1,8]{0,1,2:T(1,128)}), f32[1024,1,256]{0,1,2:T(1,128)}) %all-gather.3.cloned.1.call-update) | async-done | bytes 1048592 | tf_op jit(solution)/shard_map/all_gather | solution.py:97
  339.0 3.1 fusion.48
  342.9 1.3 convolution_bitcast_fusion
  344.3 1.3 convolution_bitcast_fusion.1
  348.7 23.5 %custom-call.16 = f32[2,128,128]{2,1,0:T(8,128)S(1)} custom-call(f32[2,128,128]{2,1,0:T(8,128)S(1)} %cholesky.122), custom_call_target="Cholesky" | custom-call | tf_op jit(solution)/shard_map/jit(cholesky)/cholesky | solution.py:33
  372.2 19.7 %custom-call.17 = f32[2,1,128,128]{2,3,1,0:T(8,128)S(1)} custom-call(f32[2,1,128,128]{3,2,1,0:T(8,128)S(1)} %select_bitcast_fusion), custom_call_target="InvertDiagBlocksLowerTriangular" | custom-call | tf_op jit(solution)/shard_map/jit(cholesky)/cholesky | solution.py:33
  393.1 1.3 convolution_subtract_fusion.2
  394.4 23.7 %custom-call.18 = f32[2,128,128]{2,1,0:T(8,128)S(1)} custom-call(f32[2,128,128]{2,1,0:T(8,128)S(1)} %convolution_subtract_fusion.2), custom_call_target="Cholesky" | custom-call | tf_op jit(solution)/shard_map/jit(cholesky)/cholesky | solution.py:33
  418.5 2.2 collective-permute-start
  420.8 4.0 while.4
  421.4 1.4 bitcast_dynamic-update-slice_fusion.4
  423.4 1.4 bitcast_dynamic-update-slice_fusion.4
  425.4 20.5 %custom-call.20 = f32[2,128,128]{1,2,0:T(8,128)S(1)} custom-call(f32[2,128,128]{2,1,0:T(8,128)} %copy-done.3), custom_call_target="InvertDiagBlocksLowerTriangular" | custom-call | tf_op jit(solution)/shard_map/triangular_solve/custom-call.0 | solution.py:34
  448.0 4.0 while.5
  448.6 1.4 bitcast_dynamic-update-slice_fusion.5
  450.6 1.4 bitcast_dynamic-update-slice_fusion.5
  452.0 19.7 %custom-call.21 = f32[2,128,128]{1,2,0:T(8,128)S(1)} custom-call(f32[2,128,128]{2,1,0:T(8,128)S(1)} %get-tuple-element.18), custom_call_target="InvertDiagBlocksLowerTriangular" | custom-call | tf_op jit(solution)/shard_map/triangular_solve/custom-call.0 | solution.py:37
  474.1 2.3 convolution_bitcast_fusion.2
  (77 shorter events, 19.6 us)
Async XLA Ops:
  7.2 41.8 %copy-start = (f32[1,512,512]{2,1,0:T(8,128)S(1)}, f32[1,512,512]{2,1,0:T(8,128)}, u32[]{:S(2)}) copy-start(f32[1,512,512]{2,1,0:T(8,128)} %param.8) | copy-start | bytes 3145732
  7.2 14.0 %copy-start.4 = (s32[4,4]{1,0:T(4,128)S(1)}, s32[4,4]{1,0:T(4,128)}, u32[]{:S(2)}) copy-start(s32[4,4]{1,0:T(4,128)} %param.10) | copy-start | bytes 196
  9.2 37.2 %all-to-all-start = ((f32[16,1024,16]{1,2,0:T(8,128)}), f32[16,1024,16]{1,2,0:T(8,128)S(1)}, u32[]{:S(2)}, u32[]{:S(2)}) async-start(f32[16,1024,16]{1,2,0:T(8,128)} %stack.14), calls=%async_computation | async-start | bytes 2097152 | tf_op jit(solution)/shard_map/all_to_all | solution.py:64
  21.1 147.5 %all-reduce.4.cloned.1.call-start = ((), (), s32[]{:S(2)}) async-start(), calls=%async_computation.6 | async-start | bytes 1048576
  53.2 176.4 %reduce-scatter.3.cloned.1.call-start = ((), (), s32[]{:S(2)}) async-start(), calls=%async_computation.3 | async-start | bytes 557056 | tf_op jit(solution)/shard_map/reduce_scatter | solution.py:80
  58.4 193.6 %reduce-scatter.5.cloned.1.call-start = ((), (), s32[]{:S(2)}) async-start(), calls=%async_computation.4 | async-start | bytes 98304 | tf_op jit(solution)/shard_map/reduce_scatter | solution.py:90
  231.8 107.2 %all-gather.3.cloned.1.call-start = ((), (), s32[]{:S(2)}) async-start(), calls=%async_computation.5 | async-start | bytes 1081344 | tf_op jit(solution)/shard_map/all_gather | solution.py:97
  347.9 0.8 copy-start.2
  418.5 55.6 %collective-permute-start = (f32[2,256,256]{2,1,0:T(8,128)S(1)}, f32[2,256,256]{2,1,0:T(8,128)}, u32[]{:S(2)}, u32[]{:S(2)}) collective-permute-start(f32[2,256,256]{2,1,0:T(8,128)S(1)} %select_select_fusion), channel_id=1, source_target_pairs={{0,16},{16,0},{32,48},{48,32},{64,80},{80,64},{96,112},{112,96},{1... | collective-permute-start | bytes 1572872 | tf_op jit(solution)/shard_map/ppermute | solution.py:18
  424.7 0.7 copy-start.3
  425.4 20.5 %copy-start.1 = (f32[256,256]{1,0:T(8,128)}, f32[256,256]{1,0:T(8,128)S(1)}, u32[]{:S(2)}) copy-start(f32[256,256]{1,0:T(8,128)S(1)} %get-tuple-element.163) | copy-start | bytes 786436
Sparse Core Ops, SparseCore 0:
  53.4 115.2 all-reduce.3
  171.6 57.9 reduce-scatter.2
  232.4 19.4 reduce-scatter.4
  255.7 83.2 all-gather.2
